TPU v7x, 32 devices: a whole 2x2x4 slice. The times are simulated.
32 devices in a mesh: parts: 2 (over x), dp: 16 (over z, y, core).
Axes of the slice: x: 2, y: 2, z: 4, core: 2. Of those that a mesh axis runs over, the one named last changes fastest.
Arguments:
- student_hidden: bfloat16 [4096, 3584], P(('parts', 'dp')), parts along dimension 0, may hold values from -6 to 6
- teacher_rows: bfloat16 [6144, 4096], P(('parts', 'dp')), parts along dimension 0, may hold values from -6 to 6
- teacher_of_row: int32 [4096, 1], P(('parts', 'dp')), parts along dimension 0, may hold values from 0 to 15; in each aligned block of 128 rows (0 to 127, 128 to 255, ...) at most 12 rows name the same one
- teacher_gain: float32 [4096], replicated, may hold values from 0.1 to 1.9
- proj_in: bfloat16 [3584, 192], replicated, may hold values from -0.09375 to 0.09375
- proj_out: bfloat16 [192, 4096], replicated, may hold values from -0.4375 to 0.4375
Outputs:
- grad_in: float32 [7168, 192], P(('parts', 'dp')), parts along dimension 0
- grad_out: float32 [384, 4096], P(('parts', 'dp')), parts along dimension 0
- row_loss: bfloat16 [4096], P(('parts', 'dp')), parts along dimension 0
There are 2 independent parts, one for each index of `parts`. A program takes and returns all parts, laid end to end along the dimension named above; an argument that names none is the same for every part. Nothing has to cross between parts.
Inputs may be any that keep to these rules, and one draw needn't show every extreme that they name: `teacher_of_row`: among the 128 rows of one device, each teacher device is named by at most 12 rows.
All inputs are finite; a program needn't handle non-finite values.
Results may differ from a plain program's by a relative error of at most 0.0038.
Values may be sent and summed in bfloat16 or wider, within the bound.
A program may use at most 64 MiB of HBM per device.

v0:
```python
import math

import jax
import jax.numpy as jnp
from jax import lax
from jax.sharding import PartitionSpec as P


def teacher_target(teacher_rows, teacher_gain):
    values = teacher_rows.astype(jnp.float32)
    scale = lax.rsqrt(jnp.mean(values * values, axis=1, keepdims=True) + 1e-06)
    return (values * scale * teacher_gain).astype(jnp.bfloat16)


def over_rows(left, right):
    return lax.dot_general(
        left, right, (((0,), (0,)), ((), ())), preferred_element_type=jnp.float32
    )


def local(student_hidden, teacher_rows, teacher_of_row, teacher_gain, proj_in, proj_out):
    peers = lax.axis_size("dp")
    tok_rows = student_hidden.shape[0]
    capacity = teacher_rows.shape[0] // peers
    window = teacher_rows.shape[1]
    factor = 1.0 / math.sqrt(tok_rows * peers)
    owner = teacher_of_row[:, 0]
    onehot = (owner[:, None] == jnp.arange(peers, dtype=jnp.int32)[None, :]).astype(jnp.int32)
    rank = jnp.sum(jnp.cumsum(onehot, axis=0) * onehot, axis=1) - 1
    slot = owner * capacity + rank
    latent = jnp.dot(student_hidden, proj_in, preferred_element_type=jnp.float32).astype(
        jnp.bfloat16
    )
    target = teacher_target(teacher_rows, teacher_gain)
    arrived = lax.all_to_all(
        target.reshape(peers, capacity, window), "dp", split_axis=0, concat_axis=0, tiled=True
    )
    matched = jnp.take(arrived.reshape(peers * capacity, window), slot, axis=0)
    pred = jnp.dot(latent, proj_out, preferred_element_type=jnp.float32)
    diff = pred - matched.astype(jnp.float32)
    row_loss = jnp.mean(diff * diff, axis=1).astype(jnp.bfloat16)
    err = (diff * factor).astype(jnp.bfloat16)
    latent_grad = lax.dot_general(
        err, proj_out, (((1,), (1,)), ((), ())), preferred_element_type=jnp.float32
    ).astype(jnp.bfloat16)
    grad_out = lax.psum_scatter(over_rows(latent, err), "dp", scatter_dimension=0, tiled=True)
    grad_in = lax.psum_scatter(
        over_rows(student_hidden, latent_grad), "dp", scatter_dimension=0, tiled=True
    )
    return (grad_in, grad_out, row_loss)


def solution(mesh):
    in_specs = (
        P(("parts", "dp"), None),
        P(("parts", "dp"), None),
        P(("parts", "dp"), None),
        P(),
        P(),
        P(),
    )
    out_specs = (P(("parts", "dp"), None), P(("parts", "dp"), None), P(("parts", "dp")))
    return jax.shard_map(local, mesh=mesh, in_specs=in_specs, out_specs=out_specs, check_vma=False)
```

profile of v0, /device:TPU:15, one launch (start us, length us, event | category | flops | bytes accessed | tf_op | source)
XLA Modules:
  0.0 196.5 jit_solution(8622091936604989011)
XLA Ops:
  7.2 0.0 copy-start
  7.2 0.0 copy-start.1
  7.2 2.0 fusion.1
  9.2 0.0 copy-done.1
  9.2 1.2 fusion.3
  10.4 1.5 reshape.35
  11.9 0.0 copy-start.6
  11.9 0.0 copy-start.2
  11.9 6.7 %all-to-all-start = ((bf16[16,12,4096]{2,1,0:T(8,128)(2,1)}), bf16[16,12,4096]{2,1,0:T(8,128)(2,1)}, u32[]{:S(2)}, u32[]{:S(2)}) async-start(bf16[16,12,4096]{2,1,0:T(8,128)(2,1)} %reshape.35), calls=%async_computation | async-start | bytes 4194304 | tf_op jit(solution)/shard_map/all_to_all | solution.py:35
  18.6 0.0 reduce-scatter.6.cloned.1.call-start
  18.6 0.0 copy-done.6
  18.6 0.1 fusion.5
  18.7 0.2 reduce_window_sum.11
  18.9 0.2 select_reduce_fusion
  19.1 0.0 copy-done.2
  19.1 1.9 convolution_convert_fusion
  21.0 45.1 %all-to-all-done = bf16[16,12,4096]{2,1,0:T(8,128)(2,1)} async-done(((bf16[16,12,4096]{2,1,0:T(8,128)(2,1)}), bf16[16,12,4096]{2,1,0:T(8,128)(2,1)}, u32[]{:S(2)}, u32[]{:S(2)}) %all-to-all-start) | async-done | bytes 1572896 | tf_op jit(solution)/shard_map/all_to_all | solution.py:35
  66.1 2.5 %reshape.36 = bf16[192,4096]{1,0:T(8,128)(2,1)S(1)} reshape(bf16[16,12,4096]{2,1,0:T(8,128)(2,1)} %all-to-all-done) | data formatting | bytes 3145728 | tf_op jit(solution)/shard_map/reshape | solution.py:38
  68.5 2.2 %gather_fusion = bf16[128,4096]{1,0:T(8,128)(2,1)} fusion(bf16[192,4096]{1,0:T(8,128)(2,1)S(1)} %reshape.36, s32[1024]{0:T(1024)S(1)} %pad_clamp_fusion), kind=kCustom, calls=%fused_computation | custom fusion | bytes 2097664 | tf_op jit(solution)/shard_map/jit(_take)/gather | solution.py:38
  70.7 0.0 copy-done
  70.7 0.0 copy-start.3
  70.7 3.3 %multiply_reduce_fusion = (f32[128]{0:T(128)S(1)}, f32[128,4096]{1,0:T(8,128)}) fusion(bf16[128,4096]{1,0:T(8,128)(2,1)} %gather_fusion, pred[128]{0:T(512)(128)(4,1)S(1)} %get-tuple-element.3, bf16[128,192]{0,1:T(8,128)(2,1)S(1)} %convolution_convert_fusion, bf16[192,4096]{1,0:T(8,128)(2,1)S(1)} %copy-done), kind=kOutput, calls=%fused_computation.8 | convolution fusion | flops 203947904 | bytes 4768384 | tf_op jit(solution)/shard_map/dot_general | solution.py:39
  74.1 0.0 copy-done.3
  74.1 4.8 %convolution_bitcast_fusion = f32[3584,192]{0,1:T(8,128)} fusion(bf16[128,3584]{1,0:T(8,128)(2,1)S(1)} %copy-done.3, bf16[192,4096]{1,0:T(8,128)(2,1)S(1)} %copy-done, f32[128,4096]{1,0:T(8,128)} %get-tuple-element.6), kind=kOutput, calls=%fused_computation.1 | convolution fusion | flops 378560512 | bytes 7340032 | tf_op jit(solution)/shard_map/dot_general | solution.py:16
  78.9 4.7 %copy.9 = f32[3584,192]{1,0:T(8,128)} copy(f32[3584,192]{0,1:T(8,128)} %convolution_bitcast_fusion) | data formatting | bytes 5505024
  83.6 0.0 reduce-scatter.6.cloned.1.call-update
  83.6 3.8 %fusion.4 = f32[192,4096]{1,0:T(8,128)} fusion(bf16[128,192]{0,1:T(8,128)(2,1)S(1)} %convolution_convert_fusion, f32[128,4096]{1,0:T(8,128)} %get-tuple-element.6), kind=kOutput, calls=%fused_computation.12 | convolution fusion | flops 202375168 | bytes 5292032 | tf_op jit(solution)/shard_map/dot_general | solution.py:16
  87.5 0.0 copy-start.7
  87.5 58.1 %fusion = f32[16,4096]{1,0:T(8,128)S(1)} fusion(f32[192,4096]{1,0:T(8,128)} %fusion.4), kind=kCustom, calls=%all-reduce-scatter | all-reduce-scatter fusion | flops 1048577 | bytes 3408384
  145.5 5.2 %collective-permute-start = (f32[16,4096]{1,0:T(8,128)S(1)}, f32[16,4096]{1,0:T(8,128)S(1)}, u32[]{:S(2)}, u32[]{:S(2)}) collective-permute-start(f32[16,4096]{1,0:T(8,128)S(1)} %fusion), channel_id=1, source_target_pairs={{0,1},{1,2},{2,3},{3,4},{4,5},{5,6},{6,7},{7,8},{8,9},{9,10},{10,1... | collective-permute-start | bytes 786440
  150.7 1.9 collective-permute-start.1
  152.6 3.1 %collective-permute-start.2 = (f32[16,4096]{1,0:T(8,128)S(1)}, f32[16,4096]{1,0:T(8,128)}, u32[]{:S(2)}, u32[]{:S(2)}) collective-permute-start(f32[16,4096]{1,0:T(8,128)S(1)} %fusion), channel_id=1, source_target_pairs={{0,3},{1,4},{2,5},{3,6},{4,7},{5,8},{6,9},{7,10},{8,11},{9,12},{10... | collective-permute-start | bytes 786440
  155.7 0.0 copy-done.7
  155.7 0.6 dynamic-slice.4
  157.0 1.9 collective-permute-start.3
  158.9 0.5 multiply_convert_fusion.4
  159.4 20.9 %collective-permute-done.3 = f32[12,4096]{1,0:T(8,128)S(1)} collective-permute-done((f32[12,4096]{1,0:T(8,128)S(1)}, f32[12,4096]{1,0:T(8,128)S(1)}, u32[]{:S(2)}, u32[]{:S(2)}) %collective-permute-start.3) | collective-permute-done | bytes 196640
  180.3 0.0 copy-start.5
  180.3 0.0 collective-permute-done
  180.3 0.0 collective-permute-done.1
  180.3 0.7 copy-done.5
  181.0 0.0 copy-start.4
  181.0 0.7 copy-done.4
  181.7 0.0 collective-permute-done.2
  181.7 5.5 %concatenate = f32[76,4096]{1,0:T(8,128)S(1)} concatenate(f32[12,4096]{1,0:T(8,128)} %copy-done.5, f32[16,4096]{1,0:T(8,128)} %collective-permute-done.2, f32[16,4096]{1,0:T(8,128)} %copy-done.4, f32[16,4096]{1,0:T(8,128)S(1)} %collective-permute-done, f32[16,4096]{1,0:T(8,128)S(1)} %fusion), dimensions={0} | concatenate | bytes 2490368
  187.2 0.7 constant_dynamic-slice_fusion
  188.0 0.0 reduce-scatter.6.cloned.1.call-done
  188.0 1.7 copy.10
  (4 shorter events, 0.0 us)
Async XLA Ops:
  7.2 63.6 %copy-start = (bf16[192,4096]{1,0:T(8,128)(2,1)S(1)}, bf16[192,4096]{1,0:T(8,128)(2,1)}, u32[]{:S(2)}) copy-start(bf16[192,4096]{1,0:T(8,128)(2,1)} %param.11) | copy-start | bytes 4718596
  7.2 2.0 %copy-start.1 = (bf16[192,4096]{1,0:T(8,128)(2,1)S(1)}, bf16[192,4096]{1,0:T(8,128)(2,1)}, u32[]{:S(2)}) copy-start(bf16[192,4096]{1,0:T(8,128)(2,1)} %param.7) | copy-start | bytes 4718596
  11.9 6.7 %copy-start.6 = (s32[128,1]{0,1:T(1,128)S(1)}, s32[128,1]{0,1:T(1,128)}, u32[]{:S(2)}) copy-start(s32[128,1]{0,1:T(1,128)} %param.8) | copy-start | bytes 1540
  11.9 7.2 %copy-start.2 = (bf16[128,3584]{1,0:T(8,128)(2,1)S(1)}, bf16[128,3584]{1,0:T(8,128)(2,1)}, u32[]{:S(2)}) copy-start(bf16[128,3584]{1,0:T(8,128)(2,1)} %param.6) | copy-start | bytes 2752516
  11.9 54.2 %all-to-all-start = ((bf16[16,12,4096]{2,1,0:T(8,128)(2,1)}), bf16[16,12,4096]{2,1,0:T(8,128)(2,1)}, u32[]{:S(2)}, u32[]{:S(2)}) async-start(bf16[16,12,4096]{2,1,0:T(8,128)(2,1)} %reshape.35), calls=%async_computation | async-start | bytes 4194304 | tf_op jit(solution)/shard_map/all_to_all | solution.py:35
  18.6 169.4 %reduce-scatter.6.cloned.1.call-start = ((), (), s32[]{:S(2)}) async-start(), calls=%async_computation.2 | async-start | bytes 3899392
  70.7 3.3 %copy-start.3 = (bf16[128,3584]{1,0:T(8,128)(2,1)S(1)}, bf16[128,3584]{1,0:T(8,128)(2,1)}, u32[]{:S(2)}) copy-start(bf16[128,3584]{1,0:T(8,128)(2,1)} %param.6) | copy-start | bytes 2752516
  87.5 68.2 %copy-start.7 = (u32[32]{0:T(128)S(1)}, u32[32]{0:T(128)}, u32[]{:S(2)}) copy-start(u32[32]{0:T(128)} %constant.39) | copy-start | bytes 388
  145.5 34.8 %collective-permute-start = (f32[16,4096]{1,0:T(8,128)S(1)}, f32[16,4096]{1,0:T(8,128)S(1)}, u32[]{:S(2)}, u32[]{:S(2)}) collective-permute-start(f32[16,4096]{1,0:T(8,128)S(1)} %fusion), channel_id=1, source_target_pairs={{0,1},{1,2},{2,3},{3,4},{4,5},{5,6},{6,7},{7,8},{8,9},{9,10},{10,1... | collective-permute-start | bytes 786440
  150.7 29.6 %collective-permute-start.1 = (f32[16,4096]{1,0:T(8,128)S(1)}, f32[16,4096]{1,0:T(8,128)S(1)}, u32[]{:S(2)}, u32[]{:S(2)}) collective-permute-start(f32[16,4096]{1,0:T(8,128)S(1)} %fusion), channel_id=1, source_target_pairs={{0,2},{1,3},{2,4},{3,5},{4,6},{5,7},{6,8},{7,9},{8,10},{9,11},{10,... | collective-permute-start | bytes 786440
  152.6 29.1 %collective-permute-start.2 = (f32[16,4096]{1,0:T(8,128)S(1)}, f32[16,4096]{1,0:T(8,128)}, u32[]{:S(2)}, u32[]{:S(2)}) collective-permute-start(f32[16,4096]{1,0:T(8,128)S(1)} %fusion), channel_id=1, source_target_pairs={{0,3},{1,4},{2,5},{3,6},{4,7},{5,8},{6,9},{7,10},{8,11},{9,12},{10... | collective-permute-start | bytes 786440
  157.0 23.3 %collective-permute-start.3 = (f32[12,4096]{1,0:T(8,128)S(1)}, f32[12,4096]{1,0:T(8,128)S(1)}, u32[]{:S(2)}, u32[]{:S(2)}) collective-permute-start(f32[12,4096]{1,0:T(8,128)S(1)} %slice.2), channel_id=1, source_target_pairs={{0,4},{1,5},{2,6},{3,7},{4,8},{5,9},{6,10},{7,11},{8,12},{9,13},{1... | collective-permute-start | bytes 589832
  180.3 0.7 copy-start.5
  181.0 0.7 copy-start.4
Sparse Core Ops, SparseCore 0:
  83.7 84.9 reduce-scatter.5
where the time goes:
time: 197 us
  waiting for transfers between devices  66 us (34%)
  blocking collectives  58.1 us (29%)
  local copies, waits for them, and re-layouts  20.9 us (11%)
  starting transfers between devices  18.8 us (10%)
  between operations  14.8 us (8%)
  matrix products  13.9 us (7%)
  other arithmetic  4.1 us (2%)
    unnamed x1, blocking collectives  58.1 us
    all_to_all x1, waiting for transfers between devices, local(): lax.all_to_all(target.reshape(peers, capacity, window), 'dp', split_axis=...  45.1 us
    unnamed x6, waiting for transfers between devices  20.9 us
    unnamed x22, local copies, waits for them, and re-layouts  14.7 us
    unnamed x5, starting transfers between devices  12.1 us
    dot_general x2, matrix products, over_rows(): lax.dot_general(left, right, (((0,), (0,)), ((), ())), preferred_element_...  8.67 us
    all_to_all x1, starting transfers between devices, local(): lax.all_to_all(target.reshape(peers, capacity, window), 'dp', split_axis=...  6.69 us
  transfers between devices with their start and end apart: 6, of which 2 were waited for; matrix products, arithmetic and copies ran while one was open for 36% of the time, Pallas kernels for 0%

commit v1 on v0

v1 whole, which is shorter than its diff:
```python
import functools
import math

import jax
import jax.numpy as jnp
from jax import lax
from jax.experimental import pallas as pl
from jax.experimental.pallas import tpu as pltpu
from jax.sharding import PartitionSpec as P

F32 = jnp.float32
BF16 = jnp.bfloat16
MESH = pl.DeviceIdType.MESH
SLOT = 16


def flip(index, bits):
    weight = 1
    while bits:
        if bits % 2:
            index = index + (1 - 2 * ((index // weight) % 2)) * weight
        bits //= 2
        weight *= 2
    return index


def nt(left, right):
    return lax.dot_general(left, right, (((1,), (1,)), ((), ())), preferred_element_type=F32)


def tn(left, right):
    return lax.dot_general(left, right, (((0,), (0,)), ((), ())), preferred_element_type=F32)


def nn(left, right):
    return jnp.dot(left, right, preferred_element_type=F32)


def ones_where(condition):
    return jnp.where(condition, 1.0, 0.0).astype(BF16)


def iota(shape, dim):
    return lax.broadcasted_iota(jnp.int32, shape, dim)


def out_plan(rows):
    if rows == 12:
        places = [(0, 12, 0)] + [(4 * q, 4, 12) for q in range(3)]
        return places, [[(q, 0), (3, q + 1)] for q in range(3)]
    if 4 * rows <= SLOT:
        return [(0, rows, rows * s) for s in range(4)], [[(s, s) for s in range(4)]]
    return [(0, rows, 0)], [[(s, 0)] for s in range(4)]


def kernel(
    cfg, student_hbm, teacher_hbm, owner_ref, gain_ref, pin_hbm, pout_hbm,
    gin_ref, gout_ref, loss_ref,
    student, teacher, pin, pout, load_sem,
    lat, snd, rcv, snd2, rcv2, studT, err, ret,
    ga_s, ga_r, gacc, gb_s, gb_r, gc_s, gc_r,
    ia_s, ia_r, iacc, ib_s, ib_r, ic_s, ic_r,
    x_ss, x_rs, y_ss, y_rs, a_ss, a_rs, b_ss, b_rs, c_ss, c_rs,
):
    peers, cap, rank_in = cfg["peers"], cfg["cap"], cfg["rank"]
    half, depth = peers // 2, peers // 4
    tok, width = student.shape
    slots, window = teacher.shape
    all_slots = peers * SLOT
    factor = 1.0 / math.sqrt(tok * peers)
    me = lax.axis_index("dp")

    loads = [
        pltpu.make_async_copy(src, dst, load_sem.at[n])
        for n, (src, dst) in enumerate(
            [(student_hbm, student), (pin_hbm, pin), (teacher_hbm, teacher), (pout_hbm, pout)]
        )
    ]
    for load in loads:
        load.start()

    barrier = pltpu.get_barrier_semaphore()

    @pl.loop(1, peers)
    def _(k):
        pl.semaphore_signal(
            barrier, inc=1, device_id={"dp": lax.rem(me + k, peers)}, device_id_type=MESH
        )

    owner = owner_ref[...]
    onehot = ones_where(owner == iota((tok, peers), 1))
    upto = ones_where(iota((tok, tok), 1) <= iota((tok, tok), 0))
    rank = jnp.sum(nn(upto, onehot) * onehot.astype(F32), axis=1, keepdims=True) - 1.0
    place = owner * SLOT + rank.astype(jnp.int32)
    pick = ones_where(place == iota((tok, all_slots), 1))

    lat[...] = jnp.zeros_like(lat)
    ret[...] = jnp.zeros_like(ret)
    loads[0].wait()
    loads[1].wait()
    lat[:, :rank_in] = nn(student[...], pin[...]).astype(BF16)
    snd[...] = tn(pick, lat[...]).astype(BF16).reshape(snd.shape)
    pl.semaphore_wait(barrier, peers - 1)

    def exchange(k, out, into, ss, rs):
        peer = lax.rem(me + k, peers)
        return pltpu.make_async_remote_copy(
            src_ref=out.at[peer], dst_ref=into.at[me], send_sem=ss.at[k], recv_sem=rs.at[k],
            device_id={"dp": peer}, device_id_type=MESH,
        )

    def arrival(k, out, into, ss, rs):
        source = lax.rem(me - k + peers, peers)
        return pltpu.make_async_remote_copy(
            src_ref=out.at[source], dst_ref=into.at[source], send_sem=ss.at[k], recv_sem=rs.at[k],
            device_id={"dp": source}, device_id_type=MESH,
        )

    def start_all(*refs):
        @pl.loop(1, peers)
        def _(k):
            exchange(k, *refs).start()

    def wait_all(*refs):
        @pl.loop(1, peers)
        def _(k):
            arrival(k, *refs).wait_recv()

    def drain_all(*refs):
        @pl.loop(1, peers)
        def _(k):
            exchange(k, *refs).wait_send()

    go = (snd, rcv, x_ss, x_rs)
    start_all(*go)
    rcv[me] = snd[me]

    loads[2].wait()
    piece = window // 8
    total = jnp.zeros((slots, 1), F32)
    for c in range(8):
        v = teacher[:, c * piece:(c + 1) * piece].astype(F32)
        total += jnp.sum(v * v, axis=1, keepdims=True)
    scale = lax.rsqrt(total * (1.0 / window) + 1e-06)
    for c in range(8):
        cols = slice(c * piece, (c + 1) * piece)
        teacher[:, cols] = (teacher[:, cols].astype(F32) * scale * gain_ref[:, cols]).astype(BF16)
    in_rows = width // peers
    if studT.shape[1] == in_rows and (width // 7) % 128 == 0:
        step = width // 7
        for c in range(7):
            turn = student[:, c * step:(c + 1) * step].T
            for r in range(0, step, SLOT):
                d, low = divmod(c * step + r, in_rows)
                studT[d, low:low + SLOT, :] = turn[r:r + SLOT, :]
    else:
        studT[...] = jnp.zeros_like(studT)
        flat = student[...].astype(F32).T
        for d in range(peers):
            studT[d, :in_rows, :] = flat[d * in_rows:(d + 1) * in_rows, :].astype(BF16)
    col = iota((slots, all_slots), 1)
    packed = ones_where((iota((slots, all_slots), 0) == (col >> 4) * cap + (col & 15)) & ((col & 15) < cap))
    row = iota((all_slots, slots), 0)
    spread = ones_where((iota((all_slots, slots), 1) == (row >> 4) * cap + (row & 15)) & ((row & 15) < cap))
    out_rows = rank_in // peers
    places, plan = out_plan(out_rows)
    row = iota((all_slots, 1), 0)
    pos, entry = row // SLOT, row % SLOT
    rest = pos % half
    dest = ((rest % depth) * 4 + (rest // depth) * 2 + pos // half) ^ me
    outsel = [
        ones_where(
            (iota((all_slots, rank_in), 1) == dest * out_rows + (lo + entry - off))
            & (entry >= off) & (entry < off + n)
        )
        for lo, n, off in places
    ]
    loads[3].wait()
    wait_all(*go)

    latents = nn(packed, rcv[...].reshape(all_slots, lat.shape[1]))[:, :rank_in].astype(BF16)
    grad = jnp.zeros((slots, rank_in), F32)
    total = jnp.zeros((slots, 1), F32)
    for c in range(8):
        cols = slice(c * piece, (c + 1) * piece)
        diff = nn(latents, pout[:, cols]) - teacher[:, cols].astype(F32)
        total += jnp.sum(diff * diff, axis=1, keepdims=True)
        e = (diff * factor).astype(BF16)
        err[:, cols] = e
        grad += nt(e, pout[:, cols])
    ret[:, :rank_in] = grad.astype(BF16)
    ret[:, rank_in:rank_in + 1] = (total * (1.0 / window)).astype(BF16)
    snd2[...] = nn(spread, ret[...]).astype(BF16).reshape(snd2.shape)
    back = (snd2, rcv2, y_ss, y_rs)
    start_all(*back)
    rcv2[me] = snd2[me]

    jobs = len(plan)

    def send(src, dst, ss, rs, bits):
        return pltpu.make_async_remote_copy(
            src_ref=src, dst_ref=dst, send_sem=ss, recv_sem=rs,
            device_id={"dp": flip(me, bits)}, device_id_type=MESH,
        )

    def refs(j):
        if j < jobs:
            return [r.at[j] for r in (ga_s, ga_r, gacc, gb_s, gb_r, gc_s, gc_r)]
        return [ia_s, ia_r, iacc, ib_s, ib_r, ic_s, ic_r]

    def copy_a(j):
        r = refs(j)
        return send(r[0], r[1], a_ss.at[j], a_rs.at[j], 1)

    def copy_b(j):
        r = refs(j)
        return send(r[3], r[4], b_ss.at[j], b_rs.at[j], 2)

    def copy_c(j, z):
        r = refs(j)
        return send(r[5].at[z - 1], r[6].at[z - 1], c_ss.at[j, z], c_rs.at[j, z], 4 * z)

    def after_a(j):
        a_s, a_r, acc, b_s, b_r, c_s, c_r = refs(j)
        copy_a(j).wait_recv()
        for h in range(depth, half):
            b_s[h - depth] = (acc[h] + a_r[h].astype(F32)).astype(BF16)
        copy_b(j).start()
        for h in range(depth):
            acc[h] = acc[h] + a_r[h].astype(F32)

    def after_b(j):
        a_s, a_r, acc, b_s, b_r, c_s, c_r = refs(j)
        copy_b(j).wait_recv()
        for z in range(depth - 1, 0, -1):
            c_s[z - 1] = (acc[z] + b_r[z].astype(F32)).astype(BF16)
            copy_c(j, z).start()
        acc[0] = acc[0] + b_r[0].astype(F32)

    def after_c(j):
        a_s, a_r, acc, b_s, b_r, c_s, c_r = refs(j)
        total = acc[0]
        for z in range(1, depth):
            copy_c(j, z).wait_recv()
            total += c_r[z - 1].astype(F32)
        return total

    turned = [nt(s, latents).astype(BF16) for s in outsel]
    chunk = window // 4
    for j, terms in enumerate(plan):
        for first in (half * SLOT, 0):
            part = sum(
                nn(turned[p][first:first + half * SLOT], err[:, s * chunk:(s + 1) * chunk])
                for s, p in terms
            )
            if first:
                ga_s[j] = part.astype(BF16).reshape(half, SLOT, chunk)
                copy_a(j).start()
            else:
                gacc[j] = part.reshape(half, SLOT, chunk)
    after_a(0)

    wait_all(*back)
    picked = nn(pick, rcv2[...].reshape(all_slots, lat.shape[1]))
    last = picked[:, 128:]
    loss_ref[...] = last.T[rank_in - 128:rank_in - 127, :].astype(BF16)
    lane = iota((tok, 128), 1) < 64
    right = jnp.where(lane, last, pltpu.roll(last, 64, 1)).astype(BF16)
    left = picked[:, :128].astype(BF16)
    whole_rows = studT.shape[1]
    split = whole_rows // 2
    low = iota((split, 128), 1) < 64
    for dc in (1, 0):
        for h in range(half):
            source = studT[flip(me, (h % depth) * 4 + (h // depth) * 2 + dc)]
            one = nn(source, left)
            two = nn(source, right)
            two = jnp.where(low, two[:split], two[split:])
            if dc:
                ia_s[h, :whole_rows, :] = one.astype(BF16)
                ia_s[h, whole_rows:, :] = two.astype(BF16)
            else:
                iacc[h, :whole_rows, :] = one
                iacc[h, whole_rows:, :] = two
        if dc:
            copy_a(jobs).start()
    for j in range(1, jobs + 1):
        after_a(j)
    for j in range(jobs + 1):
        after_b(j)
    for j, terms in enumerate(plan):
        total = after_c(j)
        for s, p in terms:
            lo, n, off = places[p]
            gout_ref[lo:lo + n, s * chunk:(s + 1) * chunk] = total[off:off + n]
    total = after_c(jobs)
    gin_ref[:, :128] = total[:in_rows]
    two = total[whole_rows:]
    gin_ref[:split, 128:] = two[:, :64]
    gin_ref[split:, 128:] = pltpu.roll(two, 64, 1)[:in_rows - split, :64]

    drain_all(*go)
    drain_all(*back)
    for j in range(jobs + 1):
        copy_a(j).wait_send()
        copy_b(j).wait_send()
        for z in range(1, depth):
            copy_c(j, z).wait_send()


def local(peers, student_hidden, teacher_rows, teacher_of_row, teacher_gain, proj_in, proj_out):
    tok, width = student_hidden.shape
    slots, window = teacher_rows.shape
    rank = proj_in.shape[1]
    padded = (rank // 128 + 1) * 128
    half, depth = peers // 2, peers // 4
    in_rows = width // peers
    in_pad = -(-in_rows // 32) * 32
    block = in_pad * 3 // 2
    out_rows = rank // peers
    jobs = len(out_plan(out_rows)[1])
    chunk = window // 4
    last = max(depth - 1, 1)
    vmem, dma = pltpu.VMEM, pltpu.SemaphoreType.DMA
    scratch = [
        vmem((tok, width), BF16), vmem((slots, window), BF16), vmem((width, rank), BF16),
        vmem((rank, window), BF16), dma((4,)),
        vmem((tok, padded), BF16),
        *[vmem((peers, SLOT, padded), BF16)] * 4,
        vmem((peers, in_pad, tok), BF16), vmem((slots, window), BF16), vmem((slots, padded), BF16),
    ]
    for lead, tile in (((jobs,), (SLOT, chunk)), ((), (block, 128))):
        scratch += [
            vmem((*lead, half, *tile), BF16), vmem((*lead, half, *tile), BF16),
            vmem((*lead, half, *tile), F32),
            vmem((*lead, depth, *tile), BF16), vmem((*lead, depth, *tile), BF16),
            vmem((*lead, last, *tile), BF16), vmem((*lead, last, *tile), BF16),
        ]
    scratch += [dma((peers,))] * 4 + [dma((jobs + 1,))] * 4 + [dma((jobs + 1, depth))] * 2
    anywhere, inside = pl.BlockSpec(memory_space=pl.ANY), pl.BlockSpec(memory_space=pltpu.VMEM)
    cfg = dict(peers=peers, cap=slots // peers, rank=rank)
    grad_in, grad_out, row_loss = pl.pallas_call(
        functools.partial(kernel, cfg),
        out_shape=(
            jax.ShapeDtypeStruct((in_rows, rank), F32),
            jax.ShapeDtypeStruct((out_rows, window), F32),
            jax.ShapeDtypeStruct((1, tok), BF16),
        ),
        in_specs=[anywhere, anywhere, inside, inside, anywhere, anywhere],
        out_specs=(inside, inside, inside),
        scratch_shapes=scratch,
        compiler_params=pltpu.CompilerParams(
            collective_id=0, has_side_effects=True, vmem_limit_bytes=56 * 2**20
        ),
    )(student_hidden, teacher_rows, teacher_of_row, teacher_gain.reshape(1, window), proj_in, proj_out)
    return grad_in, grad_out, row_loss.reshape(tok)


def solution(mesh):
    rows = P(("parts", "dp"), None)
    return jax.shard_map(
        functools.partial(local, mesh.shape["dp"]),
        mesh=mesh,
        in_specs=(rows, rows, rows, P(), P(), P()),
        out_specs=(rows, rows, P(("parts", "dp"))),
        check_vma=False,
    )
```

time: 197 us -> 56.1 us (0.28)
  the two profiles are of different devices: /device:TPU:15 before, /device:TPU:0 now
where the time goes in v1:
time: 56.1 us; the launch traced here: 55.8 us
  Pallas kernels  45.6 us (81%)
  local copies, waits for them, and re-layouts  9.56 us (17%)
  between operations  0.64 us (1%)
    pallas_call x1, Pallas kernels, local(): pl.pallas_call(functools.partial(kernel, cfg), out_shape=(jax.ShapeDtypeS...  45.6 us
    unnamed x5, local copies, waits for them, and re-layouts  9.56 us

profile of v1, /device:TPU:0, one launch (start us, length us, event | category | flops | bytes accessed | tf_op | source)
XLA Modules:
  0.0 55.8 jit_solution(8383182777595359720)
XLA Ops:
  0.6 1.4 %copy.9.owner_ref = s32[128,1]{1,0:T(8,128)} copy(s32[128,1]{0,1:T(1,128)} %param.8) | data formatting | bytes 1024 | tf_op args[2]
  2.0 3.6 %copy.10.pin_hbm = bf16[3584,192]{1,0:T(8,128)(2,1)} copy(bf16[3584,192]{0,1:T(8,128)(2,1)} %param.10) | data formatting | bytes 2752512 | tf_op args[4]
  5.6 45.6 %shard_map.85 = (f32[224,192]{1,0:T(8,128)}, f32[12,4096]{1,0:T(8,128)}, bf16[1,128]{1,0:T(2,128)(2,1)}) custom-call(bf16[128,3584]{1,0:T(8,128)(2,1)} %student_hbm.1, bf16[192,4096]{1,0:T(8,128)(2,1)} %teacher_hbm.1, s32[128,1]{1,0:T(8,128)} %copy.9.owner_ref, f32[1,4096]{1,0:T(1,128)} %bitcast.2, bf16[3584,192]{1,0:T(8,128)(2,1)} %copy.10.pin_hbm, ...), custom_call_target="tpu_custom_call" | custom-call | tf_op jit(solution)/shard_map/pallas_call | solution.py:342
  51.3 1.7 %copy.11 = f32[224,192]{0,1:T(8,128)} copy(f32[224,192]{1,0:T(8,128)} %get-tuple-element.9) | data formatting | bytes 344064
  53.0 1.7 %copy.14 = f32[12,4096]{1,0:T(8,128)} copy(f32[12,4096]{1,0:T(8,128)} %get-tuple-element.16) | data formatting | bytes 393216
  54.7 1.1 %copy.15 = bf16[128]{0:T(256)(128)(2,1)} copy(bf16[128]{0:T(256)(128)(2,1)} %bitcast.3) | data formatting | bytes 512

commit v2 on v1

--- a/solution.py
+++ b/solution.py
@@ -55,7 +55,7 @@
 
 def kernel(
     cfg, student_hbm, teacher_hbm, owner_ref, gain_ref, pin_hbm, pout_hbm,
-    gin_ref, gout_ref, loss_ref,
+    in_sum, out_sum, loss_ref,
     student, teacher, pin, pout, load_sem,
     lat, snd, rcv, snd2, rcv2, studT, err, ret,
     ga_s, ga_r, gacc, gb_s, gb_r, gc_s, gc_r,
@@ -88,18 +88,18 @@
         )
 
     owner = owner_ref[...]
-    onehot = ones_where(owner == iota((tok, peers), 1))
-    upto = ones_where(iota((tok, tok), 1) <= iota((tok, tok), 0))
-    rank = jnp.sum(nn(upto, onehot) * onehot.astype(F32), axis=1, keepdims=True) - 1.0
+    onehot = ones_where(owner == iota((peers, tok), 0))
+    upto = ones_where(iota((tok, tok), 0) <= iota((tok, tok), 1))
+    rank = jnp.sum(nn(onehot, upto) * onehot.astype(F32), axis=0, keepdims=True) - 1.0
     place = owner * SLOT + rank.astype(jnp.int32)
-    pick = ones_where(place == iota((tok, all_slots), 1))
+    pick = ones_where(place == iota((all_slots, tok), 0))
 
     lat[...] = jnp.zeros_like(lat)
     ret[...] = jnp.zeros_like(ret)
     loads[0].wait()
     loads[1].wait()
-    lat[:, :rank_in] = nn(student[...], pin[...]).astype(BF16)
-    snd[...] = tn(pick, lat[...]).astype(BF16).reshape(snd.shape)
+    lat[:, :rank_in] = nt(student[...], pin[...]).astype(BF16)
+    snd[...] = nn(pick, lat[...]).astype(BF16).reshape(snd.shape)
     pl.semaphore_wait(barrier, peers - 1)
 
     def exchange(k, out, into, ss, rs):
@@ -261,7 +261,7 @@
     after_a(0)
 
     wait_all(*back)
-    picked = nn(pick, rcv2[...].reshape(all_slots, lat.shape[1]))
+    picked = tn(pick, rcv2[...].reshape(all_slots, lat.shape[1]))
     last = picked[:, 128:]
     loss_ref[...] = last.T[rank_in - 128:rank_in - 127, :].astype(BF16)
     lane = iota((tok, 128), 1) < 64
@@ -288,16 +288,9 @@
         after_a(j)
     for j in range(jobs + 1):
         after_b(j)
-    for j, terms in enumerate(plan):
-        total = after_c(j)
-        for s, p in terms:
-            lo, n, off = places[p]
-            gout_ref[lo:lo + n, s * chunk:(s + 1) * chunk] = total[off:off + n]
-    total = after_c(jobs)
-    gin_ref[:, :128] = total[:in_rows]
-    two = total[whole_rows:]
-    gin_ref[:split, 128:] = two[:, :64]
-    gin_ref[split:, 128:] = pltpu.roll(two, 64, 1)[:in_rows - split, :64]
+    for j in range(jobs):
+        out_sum[j] = after_c(j)
+    in_sum[...] = after_c(jobs)
 
     drain_all(*go)
     drain_all(*back)
@@ -306,6 +299,23 @@
         copy_b(j).wait_send()
         for z in range(1, depth):
             copy_c(j, z).wait_send()
+
+
+def unpack(out_rows, in_sum, out_sum, loss_in, gin_ref, gout_ref, loss_ref):
+    places, plan = out_plan(out_rows)
+    chunk = out_sum.shape[2]
+    for j, terms in enumerate(plan):
+        for s, p in terms:
+            lo, n, off = places[p]
+            gout_ref[lo:lo + n, s * chunk:(s + 1) * chunk] = out_sum[j, off:off + n, :]
+    rank, in_rows = gin_ref.shape
+    whole = in_sum.shape[0] * 2 // 3
+    split = whole // 2
+    gin_ref[:128, :] = in_sum[:whole, :].T[:, :in_rows]
+    two = in_sum[whole:, :].T
+    gin_ref[128:, :split] = two[:64]
+    gin_ref[128:, split:] = two[64:, :in_rows - split]
+    loss_ref[...] = loss_in[...]
 
 
 def local(peers, student_hidden, teacher_rows, teacher_of_row, teacher_gain, proj_in, proj_out):
@@ -323,7 +333,7 @@
     last = max(depth - 1, 1)
     vmem, dma = pltpu.VMEM, pltpu.SemaphoreType.DMA
     scratch = [
-        vmem((tok, width), BF16), vmem((slots, window), BF16), vmem((width, rank), BF16),
+        vmem((tok, width), BF16), vmem((slots, window), BF16), vmem((rank, width), BF16),
         vmem((rank, window), BF16), dma((4,)),
         vmem((tok, padded), BF16),
         *[vmem((peers, SLOT, padded), BF16)] * 4,
@@ -339,11 +349,11 @@
     scratch += [dma((peers,))] * 4 + [dma((jobs + 1,))] * 4 + [dma((jobs + 1, depth))] * 2
     anywhere, inside = pl.BlockSpec(memory_space=pl.ANY), pl.BlockSpec(memory_space=pltpu.VMEM)
     cfg = dict(peers=peers, cap=slots // peers, rank=rank)
-    grad_in, grad_out, row_loss = pl.pallas_call(
+    in_sum, out_sum, row_loss = pl.pallas_call(
         functools.partial(kernel, cfg),
         out_shape=(
-            jax.ShapeDtypeStruct((in_rows, rank), F32),
-            jax.ShapeDtypeStruct((out_rows, window), F32),
+            jax.ShapeDtypeStruct((block, 128), F32),
+            jax.ShapeDtypeStruct((jobs, SLOT, chunk), F32),
             jax.ShapeDtypeStruct((1, tok), BF16),
         ),
         in_specs=[anywhere, anywhere, inside, inside, anywhere, anywhere],
@@ -352,8 +362,19 @@
         compiler_params=pltpu.CompilerParams(
             collective_id=0, has_side_effects=True, vmem_limit_bytes=56 * 2**20
         ),
-    )(student_hidden, teacher_rows, teacher_of_row, teacher_gain.reshape(1, window), proj_in, proj_out)
-    return grad_in, grad_out, row_loss.reshape(tok)
+    )(
+        student_hidden, teacher_rows, teacher_of_row.reshape(1, tok),
+        teacher_gain.reshape(1, window), proj_in.T, proj_out,
+    )
+    grad_in, grad_out, row_loss = pl.pallas_call(
+        functools.partial(unpack, out_rows),
+        out_shape=(
+            jax.ShapeDtypeStruct((rank, in_rows), F32),
+            jax.ShapeDtypeStruct((out_rows, window), F32),
+            jax.ShapeDtypeStruct((1, tok), BF16),
+        ),
+    )(in_sum, out_sum, row_loss)
+    return grad_in.T, grad_out, row_loss.reshape(tok)
 
 
 def solution(mesh):

time: 56.1 us -> 48.3 us (0.86)
  local copies, waits for them, and re-layouts: 9.56 us -> 0 us
  Pallas kernels: 45.6 us -> 47.4 us
    unnamed x5 -> x0, local copies, waits for them, and re-layouts: 9.56 us -> none
    pallas_call x0 -> x1, Pallas kernels: none -> 1.89 us  [local(): pl.pallas_call(functools.partial(unpack, out_rows), out_shape=(jax.ShapeD...]
where the time goes in v2:
time: 48.3 us; the launch traced here: 48 us
  Pallas kernels  47.4 us (98%)
  between operations  0.64 us (1%)
    pallas_call x1, Pallas kernels, local(): pl.pallas_call(functools.partial(kernel, cfg), out_shape=(jax.ShapeDtypeS...  45.5 us
    pallas_call x1, Pallas kernels, local(): pl.pallas_call(functools.partial(unpack, out_rows), out_shape=(jax.ShapeD...  1.89 us

profile of v2, /device:TPU:0, one launch (start us, length us, event | category | flops | bytes accessed | tf_op | source)
XLA Modules:
  0.0 48.0 jit_solution(3879774382432954797)
XLA Ops:
  0.6 45.5 %shard_map.85 = (f32[336,128]{1,0:T(8,128)}, f32[3,16,1024]{2,1,0:T(8,128)}, bf16[1,128]{1,0:T(2,128)(2,1)}) custom-call(bf16[128,3584]{1,0:T(8,128)(2,1)} %student_hbm.1, bf16[192,4096]{1,0:T(8,128)(2,1)} %teacher_hbm.1, s32[1,128]{1,0:T(1,128)} %bitcast.7, f32[1,4096]{1,0:T(1,128)} %bitcast.6, bf16[192,3584]{1,0:T(8,128)(2,1)} %bitcast.5, ...), custom_call_target="tpu_custom_call" | custom-call | tf_op jit(solution)/shard_map/pallas_call | solution.py:352
  46.2 1.9 %shard_map.86 = (f32[192,224]{1,0:T(8,128)}, f32[12,4096]{1,0:T(8,128)}, bf16[1,128]{1,0:T(2,128)(2,1)}) custom-call(f32[336,128]{1,0:T(8,128)} %get-tuple-element.9.in_sum, f32[3,16,1024]{2,1,0:T(8,128)} %get-tuple-element.10.out_sum, bf16[1,128]{1,0:T(2,128)(2,1)} %get-tuple-element.11.loss_in), custom_call_target="tpu_custom_call" | custom-call | tf_op jit(solution)/shard_map/pallas_call | solution.py:369

commit v3 on v2

--- a/solution.py
+++ b/solution.py
@@ -53,17 +53,26 @@
     return [(0, rows, 0)], [[(s, 0)] for s in range(4)]
 
 
+def job_orders(jobs, stages):
+    rising = tuple(1 << i for i in range(stages))
+    other = rising[:1] + rising[2:3] + rising[1:2] + rising[3:]
+    orders = [rising] * (jobs + 3)
+    orders[jobs + 1] = other
+    if jobs > 1:
+        orders[1] = other
+    return orders
+
+
 def kernel(
     cfg, student_hbm, teacher_hbm, owner_ref, gain_ref, pin_hbm, pout_hbm,
     in_sum, out_sum, loss_ref,
     student, teacher, pin, pout, load_sem,
     lat, snd, rcv, snd2, rcv2, studT, err, ret,
-    ga_s, ga_r, gacc, gb_s, gb_r, gc_s, gc_r,
-    ia_s, ia_r, iacc, ib_s, ib_r, ic_s, ic_r,
-    x_ss, x_rs, y_ss, y_rs, a_ss, a_rs, b_ss, b_rs, c_ss, c_rs,
+    g_out, g_into, g_acc, i_out, i_into, i_acc,
+    x_ss, x_rs, y_ss, y_rs, j_ss, j_rs,
 ):
     peers, cap, rank_in = cfg["peers"], cfg["cap"], cfg["rank"]
-    half, depth = peers // 2, peers // 4
+    half, stages = peers // 2, peers.bit_length() - 1
     tok, width = student.shape
     slots, window = teacher.shape
     all_slots = peers * SLOT
@@ -100,7 +109,13 @@
     loads[1].wait()
     lat[:, :rank_in] = nt(student[...], pin[...]).astype(BF16)
     snd[...] = nn(pick, lat[...]).astype(BF16).reshape(snd.shape)
-    pl.semaphore_wait(barrier, peers - 1)
+
+    def each_peer(step):
+        if peers <= 16:
+            for k in sorted(range(1, peers), key=lambda k: -min(k, peers - k)):
+                step(k)
+        else:
+            pl.loop(1, peers)(step)
 
     def exchange(k, out, into, ss, rs):
         peer = lax.rem(me + k, peers)
@@ -117,23 +132,13 @@
         )
 
     def start_all(*refs):
-        @pl.loop(1, peers)
-        def _(k):
-            exchange(k, *refs).start()
+        each_peer(lambda k: exchange(k, *refs).start())
 
     def wait_all(*refs):
-        @pl.loop(1, peers)
-        def _(k):
-            arrival(k, *refs).wait_recv()
+        each_peer(lambda k: arrival(k, *refs).wait_recv())
 
     def drain_all(*refs):
-        @pl.loop(1, peers)
-        def _(k):
-            exchange(k, *refs).wait_send()
-
-    go = (snd, rcv, x_ss, x_rs)
-    start_all(*go)
-    rcv[me] = snd[me]
+        each_peer(lambda k: exchange(k, *refs).wait_send())
 
     loads[2].wait()
     piece = window // 8
@@ -145,6 +150,10 @@
     for c in range(8):
         cols = slice(c * piece, (c + 1) * piece)
         teacher[:, cols] = (teacher[:, cols].astype(F32) * scale * gain_ref[:, cols]).astype(BF16)
+    go = (snd, rcv, x_ss, x_rs)
+    pl.semaphore_wait(barrier, peers - 1)
+    start_all(*go)
+    rcv[me] = snd[me]
     in_rows = width // peers
     if studT.shape[1] == in_rows and (width // 7) % 128 == 0:
         step = width // 7
@@ -166,99 +175,86 @@
     places, plan = out_plan(out_rows)
     row = iota((all_slots, 1), 0)
     pos, entry = row // SLOT, row % SLOT
-    rest = pos % half
-    dest = ((rest % depth) * 4 + (rest // depth) * 2 + pos // half) ^ me
-    outsel = [
-        ones_where(
-            (iota((all_slots, rank_in), 1) == dest * out_rows + (lo + entry - off))
-            & (entry >= off) & (entry < off + n)
-        )
-        for lo, n, off in places
-    ]
+    jobs = len(plan)
+    orders = job_orders(jobs, stages)
+    outsel = {}
+    for j, terms in enumerate(plan):
+        dest = sum(((pos >> (stages - 1 - i)) & 1) * bit for i, bit in enumerate(orders[j])) ^ me
+        for _, p in terms:
+            lo, n, off = places[p]
+            if (orders[j], p) not in outsel:
+                outsel[orders[j], p] = ones_where(
+                    (iota((all_slots, rank_in), 1) == dest * out_rows + (lo + entry - off))
+                    & (entry >= off) & (entry < off + n)
+                )
     loads[3].wait()
     wait_all(*go)
 
     latents = nn(packed, rcv[...].reshape(all_slots, lat.shape[1]))[:, :rank_in].astype(BF16)
+    turned = {key: nt(sel, latents).astype(BF16) for key, sel in outsel.items()}
+
+    def refs(j):
+        if j < jobs:
+            return g_out.at[j], g_into.at[j], g_acc.at[j]
+        return i_out.at[j - jobs], i_into.at[j - jobs], i_acc.at[j - jobs]
+
+    def copy(j, stage):
+        out, into, _ = refs(j)
+        count = peers >> (stage + 1)
+        return pltpu.make_async_remote_copy(
+            src_ref=out.at[pl.ds(count, count)], dst_ref=into.at[pl.ds(count, count)],
+            send_sem=j_ss.at[j, stage], recv_sem=j_rs.at[j, stage],
+            device_id={"dp": flip(me, orders[j][stage])}, device_id_type=MESH,
+        )
+
+    def advance(j, stage):
+        out, into, acc = refs(j)
+        copy(j, stage).wait_recv()
+        count = peers >> (stage + 1)
+        kept = count // 2
+        if kept:
+            for h in range(kept, count):
+                out[h] = (acc[h] + into[count + h].astype(F32)).astype(BF16)
+            copy(j, stage + 1).start()
+        for h in range(max(kept, 1)):
+            acc[h] = acc[h] + into[count + h].astype(F32)
+
     grad = jnp.zeros((slots, rank_in), F32)
     total = jnp.zeros((slots, 1), F32)
-    for c in range(8):
-        cols = slice(c * piece, (c + 1) * piece)
-        diff = nn(latents, pout[:, cols]) - teacher[:, cols].astype(F32)
-        total += jnp.sum(diff * diff, axis=1, keepdims=True)
-        e = (diff * factor).astype(BF16)
-        err[:, cols] = e
-        grad += nt(e, pout[:, cols])
+    chunk = window // 4
+    ready, started = set(), []
+    for quarter in (3, 0, 1, 2):
+        for c in (2 * quarter, 2 * quarter + 1):
+            cols = slice(c * piece, (c + 1) * piece)
+            diff = nn(latents, pout[:, cols]) - teacher[:, cols].astype(F32)
+            total += jnp.sum(diff * diff, axis=1, keepdims=True)
+            e = (diff * factor).astype(BF16)
+            err[:, cols] = e
+            grad += nt(e, pout[:, cols])
+        ready.add(quarter)
+        for j, terms in enumerate(plan):
+            if j in started or not ready.issuperset(q for q, _ in terms):
+                continue
+            for first in (half * SLOT, 0):
+                part = sum(
+                    nn(turned[orders[j], p][first:first + half * SLOT], err[:, q * chunk:(q + 1) * chunk])
+                    for q, p in terms
+                )
+                if first:
+                    g_out[j, half:] = part.astype(BF16).reshape(half, SLOT, chunk)
+                    copy(j, 0).start()
+                else:
+                    g_acc[j] = part.reshape(half, SLOT, chunk)
+            if started:
+                advance(started[-1], 0)
+            started.append(j)
     ret[:, :rank_in] = grad.astype(BF16)
     ret[:, rank_in:rank_in + 1] = (total * (1.0 / window)).astype(BF16)
     snd2[...] = nn(spread, ret[...]).astype(BF16).reshape(snd2.shape)
     back = (snd2, rcv2, y_ss, y_rs)
     start_all(*back)
     rcv2[me] = snd2[me]
-
-    jobs = len(plan)
-
-    def send(src, dst, ss, rs, bits):
-        return pltpu.make_async_remote_copy(
-            src_ref=src, dst_ref=dst, send_sem=ss, recv_sem=rs,
-            device_id={"dp": flip(me, bits)}, device_id_type=MESH,
-        )
-
-    def refs(j):
-        if j < jobs:
-            return [r.at[j] for r in (ga_s, ga_r, gacc, gb_s, gb_r, gc_s, gc_r)]
-        return [ia_s, ia_r, iacc, ib_s, ib_r, ic_s, ic_r]
-
-    def copy_a(j):
-        r = refs(j)
-        return send(r[0], r[1], a_ss.at[j], a_rs.at[j], 1)
-
-    def copy_b(j):
-        r = refs(j)
-        return send(r[3], r[4], b_ss.at[j], b_rs.at[j], 2)
-
-    def copy_c(j, z):
-        r = refs(j)
-        return send(r[5].at[z - 1], r[6].at[z - 1], c_ss.at[j, z], c_rs.at[j, z], 4 * z)
-
-    def after_a(j):
-        a_s, a_r, acc, b_s, b_r, c_s, c_r = refs(j)
-        copy_a(j).wait_recv()
-        for h in range(depth, half):
-            b_s[h - depth] = (acc[h] + a_r[h].astype(F32)).astype(BF16)
-        copy_b(j).start()
-        for h in range(depth):
-            acc[h] = acc[h] + a_r[h].astype(F32)
-
-    def after_b(j):
-        a_s, a_r, acc, b_s, b_r, c_s, c_r = refs(j)
-        copy_b(j).wait_recv()
-        for z in range(depth - 1, 0, -1):
-            c_s[z - 1] = (acc[z] + b_r[z].astype(F32)).astype(BF16)
-            copy_c(j, z).start()
-        acc[0] = acc[0] + b_r[0].astype(F32)
-
-    def after_c(j):
-        a_s, a_r, acc, b_s, b_r, c_s, c_r = refs(j)
-        total = acc[0]
-        for z in range(1, depth):
-            copy_c(j, z).wait_recv()
-            total += c_r[z - 1].astype(F32)
-        return total
-
-    turned = [nt(s, latents).astype(BF16) for s in outsel]
-    chunk = window // 4
-    for j, terms in enumerate(plan):
-        for first in (half * SLOT, 0):
-            part = sum(
-                nn(turned[p][first:first + half * SLOT], err[:, s * chunk:(s + 1) * chunk])
-                for s, p in terms
-            )
-            if first:
-                ga_s[j] = part.astype(BF16).reshape(half, SLOT, chunk)
-                copy_a(j).start()
-            else:
-                gacc[j] = part.reshape(half, SLOT, chunk)
-    after_a(0)
+    advance(started[-1], 0)
 
     wait_all(*back)
     picked = tn(pick, rcv2[...].reshape(all_slots, lat.shape[1]))
@@ -270,35 +266,42 @@
     whole_rows = studT.shape[1]
     split = whole_rows // 2
     low = iota((split, 128), 1) < 64
-    for dc in (1, 0):
-        for h in range(half):
-            source = studT[flip(me, (h % depth) * 4 + (h // depth) * 2 + dc)]
-            one = nn(source, left)
-            two = nn(source, right)
-            two = jnp.where(low, two[:split], two[split:])
-            if dc:
-                ia_s[h, :whole_rows, :] = one.astype(BF16)
-                ia_s[h, whole_rows:, :] = two.astype(BF16)
-            else:
-                iacc[h, :whole_rows, :] = one
-                iacc[h, whole_rows:, :] = two
-        if dc:
-            copy_a(jobs).start()
-    for j in range(1, jobs + 1):
-        after_a(j)
-    for j in range(jobs + 1):
-        after_b(j)
+    early = [(j, 1) for j in range(min(jobs, 2))]
+    for j, t in early:
+        advance(j, t)
+    for j in range(jobs, jobs + 3):
+        out, _, acc = refs(j)
+        for core in (1, 0):
+            for h in range(half):
+                bits = orders[j][0] * core + sum(
+                    bit for i, bit in enumerate(orders[j]) if i and (h >> (stages - 1 - i)) & 1
+                )
+                source = studT[flip(me, bits)]
+                if j < jobs + 2:
+                    block = nn(source[(j - jobs) * split:(j - jobs + 1) * split], left)
+                else:
+                    block = nn(source, right)
+                    block = jnp.where(low, block[:split], block[split:])
+                if core:
+                    out[half + h] = block.astype(BF16)
+                else:
+                    acc[h] = block
+            if core:
+                copy(j, 0).start()
+    steps = [(j + 3 * t, j, t) for j in range(jobs + 3) for t in range(stages) if j >= jobs or t > 0]
+    for _, j, t in sorted(steps):
+        if (j, t) not in early:
+            advance(j, t)
     for j in range(jobs):
-        out_sum[j] = after_c(j)
-    in_sum[...] = after_c(jobs)
+        out_sum[j] = g_acc[j, 0]
+    for j in range(3):
+        in_sum[j * split:(j + 1) * split, :] = i_acc[j, 0]
 
     drain_all(*go)
     drain_all(*back)
-    for j in range(jobs + 1):
-        copy_a(j).wait_send()
-        copy_b(j).wait_send()
-        for z in range(1, depth):
-            copy_c(j, z).wait_send()
+    for j in range(jobs + 3):
+        for t in range(stages):
+            copy(j, t).wait_send()
 
 
 def unpack(out_rows, in_sum, out_sum, loss_in, gin_ref, gout_ref, loss_ref):
@@ -323,14 +326,13 @@
     slots, window = teacher_rows.shape
     rank = proj_in.shape[1]
     padded = (rank // 128 + 1) * 128
-    half, depth = peers // 2, peers // 4
+    half = peers // 2
     in_rows = width // peers
     in_pad = -(-in_rows // 32) * 32
     block = in_pad * 3 // 2
     out_rows = rank // peers
     jobs = len(out_plan(out_rows)[1])
     chunk = window // 4
-    last = max(depth - 1, 1)
     vmem, dma = pltpu.VMEM, pltpu.SemaphoreType.DMA
     scratch = [
         vmem((tok, width), BF16), vmem((slots, window), BF16), vmem((rank, width), BF16),
@@ -339,14 +341,9 @@
         *[vmem((peers, SLOT, padded), BF16)] * 4,
         vmem((peers, in_pad, tok), BF16), vmem((slots, window), BF16), vmem((slots, padded), BF16),
     ]
-    for lead, tile in (((jobs,), (SLOT, chunk)), ((), (block, 128))):
-        scratch += [
-            vmem((*lead, half, *tile), BF16), vmem((*lead, half, *tile), BF16),
-            vmem((*lead, half, *tile), F32),
-            vmem((*lead, depth, *tile), BF16), vmem((*lead, depth, *tile), BF16),
-            vmem((*lead, last, *tile), BF16), vmem((*lead, last, *tile), BF16),
-        ]
-    scratch += [dma((peers,))] * 4 + [dma((jobs + 1,))] * 4 + [dma((jobs + 1, depth))] * 2
+    for lead, tile in ((jobs, (SLOT, chunk)), (3, (in_pad // 2, 128))):
+        scratch += [vmem((lead, peers, *tile), BF16)] * 2 + [vmem((lead, half, *tile), F32)]
+    scratch += [dma((peers,))] * 4 + [dma((jobs + 3, peers.bit_length() - 1))] * 2
     anywhere, inside = pl.BlockSpec(memory_space=pl.ANY), pl.BlockSpec(memory_space=pltpu.VMEM)
     cfg = dict(peers=peers, cap=slots // peers, rank=rank)
     in_sum, out_sum, row_loss = pl.pallas_call(

time: 48.3 us -> 45.5 us (0.942)
  Pallas kernels: 47.4 us -> 44.6 us
    pallas_call x1, Pallas kernels: 45.5 us -> 42.7 us  [local(): pl.pallas_call(functools.partial(kernel, cfg), out_shape=(jax.ShapeDtypeS...]
where the time goes in v3:
time: 45.5 us; the launch traced here: 45.2 us
  Pallas kernels  44.6 us (98%)
  between operations  0.64 us (1%)
    pallas_call x1, Pallas kernels, local(): pl.pallas_call(functools.partial(kernel, cfg), out_shape=(jax.ShapeDtypeS...  42.7 us
    pallas_call x1, Pallas kernels, local(): pl.pallas_call(functools.partial(unpack, out_rows), out_shape=(jax.ShapeD...  1.89 us

profile of v3, /device:TPU:0, one launch (start us, length us, event | category | flops | bytes accessed | tf_op | source)
XLA Modules:
  0.0 45.2 jit_solution(10434820088465236454)
XLA Ops:
  0.6 42.7 %shard_map.85 = (f32[336,128]{1,0:T(8,128)}, f32[3,16,1024]{2,1,0:T(8,128)}, bf16[1,128]{1,0:T(2,128)(2,1)}) custom-call(bf16[128,3584]{1,0:T(8,128)(2,1)} %student_hbm.1, bf16[192,4096]{1,0:T(8,128)(2,1)} %teacher_hbm.1, s32[1,128]{1,0:T(1,128)} %bitcast.7, f32[1,4096]{1,0:T(1,128)} %bitcast.6, bf16[192,3584]{1,0:T(8,128)(2,1)} %bitcast.5, ...), custom_call_target="tpu_custom_call" | custom-call | tf_op jit(solution)/shard_map/pallas_call | solution.py:349
  43.3 1.9 %shard_map.86 = (f32[192,224]{1,0:T(8,128)}, f32[12,4096]{1,0:T(8,128)}, bf16[1,128]{1,0:T(2,128)(2,1)}) custom-call(f32[336,128]{1,0:T(8,128)} %get-tuple-element.9.in_sum, f32[3,16,1024]{2,1,0:T(8,128)} %get-tuple-element.10.out_sum, bf16[1,128]{1,0:T(2,128)(2,1)} %get-tuple-element.11.loss_in), custom_call_target="tpu_custom_call" | custom-call | tf_op jit(solution)/shard_map/pallas_call | solution.py:366
